TPU v7x, 32 devices: a whole 2x2x4 slice. The times are simulated.
32 devices in a mesh: pipe: 4 (over z), expert: 8 (over y, x, core).
Axes of the slice: x: 2, y: 2, z: 4, core: 2. Of those that a mesh axis runs over, the one named last changes fastest.
Arguments:
- tokens: bfloat16 [4096, 3584], P(('pipe', 'expert')), may hold values from -6 to 6
- out_grad: bfloat16 [4096, 3584], P(('pipe', 'expert')), may hold values from -6 to 6
- probs: bfloat16 [4096, 8], P(('pipe', 'expert')), may hold values from 0.049804688 to 1
- expert_ids: int32 [4096, 8], P(('pipe', 'expert')), may hold values from 0 to 255, as said below
- w_gate: bfloat16 [4, 3584, 2048], P('pipe', None, 'expert'), as said below
- w_up: bfloat16 [4, 3584, 2048], P('pipe', None, 'expert'), as said below
- w_down: bfloat16 [4, 2048, 3584], P('pipe', 'expert'), as said below
Outputs:
- tokens_grad: bfloat16 [4096, 3584], P(('pipe', 'expert'))
- weight_grads: bfloat16 [4, 3, 1792, 2048], P('pipe', None, None, 'expert')
Inputs may be any that keep to these rules, and one draw needn't show every extreme that they name: `expert_ids`: each row names 8 different experts. Experts 1 and above lie outside this window. Among the 128 tokens of one device (aligned blocks of rows), each expert below 1 is named by at most 8 tokens, and in every draw one such expert is named by exactly 8 tokens on every device. `w_gate`: entries k and 3 - k along the first dimension are equal. `w_up`: entries k and 3 - k along the first dimension are equal. `w_down`: entries k and 3 - k along the first dimension are equal.
All inputs are finite; a program needn't handle non-finite values.
Results may differ from a plain program's by a relative error of at most 0.0065.
Values may be sent and summed in bfloat16 or wider, within the bound.
A program may use at most 128 MiB of HBM per device.

v0:
```python
import jax
import jax.numpy as jnp
from jax import lax
from jax.sharding import PartitionSpec as P

GROUP = 8
CAP = 8


def from_partner(value, axis, apart):
    mask = 2**apart
    pairs = [(source, source ^ mask) for source in range(lax.axis_size(axis))]
    return lax.ppermute(value, axis, pairs)


def route_slots(block_ids, block_probs, in_flight):
    experts = jnp.arange(in_flight, dtype=jnp.int32)
    hits = block_ids[:, :, None] == experts[None, None, :]
    member = jnp.any(hits, axis=1).astype(jnp.int32)
    chosen = jnp.sum(
        jnp.where(hits, block_probs.astype(jnp.float32)[:, :, None], jnp.float32(0.0)), axis=1
    )
    position = jnp.cumsum(member, axis=0) - member
    slots = jnp.arange(CAP, dtype=jnp.int32)
    select = (member.T[:, None, :] == 1) & (position.T[:, None, :] == slots[None, :, None])
    select = select.astype(jnp.float32)
    slot_weight = jnp.einsum("ect,te->ec", select, chosen, precision=lax.Precision.HIGHEST)
    return (select.reshape(in_flight * CAP, -1), slot_weight.reshape(in_flight * CAP))


def contract(left, right, left_dim, right_dim):
    return lax.dot_general(
        left, right, (((left_dim,), (right_dim,)), ((), ())), preferred_element_type=jnp.float32
    )


def expert_backward(x_rows, grad_rows, gate_cols, up_cols, down_rows):
    gate = jnp.dot(x_rows, gate_cols, preferred_element_type=jnp.float32)
    up = jnp.dot(x_rows, up_cols, preferred_element_type=jnp.float32)
    sigmoid_gate = jax.nn.sigmoid(gate)
    activated = gate * sigmoid_gate
    hidden = (activated * up).astype(jnp.bfloat16)
    back = contract(grad_rows, down_rows, 1, 1)
    d_gate = (back * up * sigmoid_gate * (1.0 + gate * (1.0 - sigmoid_gate))).astype(jnp.bfloat16)
    d_up = (back * activated).astype(jnp.bfloat16)
    row_grad = contract(d_gate, gate_cols, 1, 1) + contract(d_up, up_cols, 1, 1)
    grads = jnp.stack(
        [
            contract(x_rows, d_gate, 0, 0),
            contract(x_rows, d_up, 0, 0),
            contract(grad_rows, hidden, 0, 0),
        ]
    ).astype(jnp.bfloat16)
    return (row_grad, grads)


def body(tokens, out_grad, probs, expert_ids, w_gate, w_up, w_down):
    axis_width = lax.axis_size("expert")
    in_flight = axis_width // GROUP
    features = tokens.shape[1]
    select, slot_weight = route_slots(expert_ids, probs, in_flight)
    picker = select.astype(jnp.bfloat16)
    x_rows = jnp.dot(picker, tokens, preferred_element_type=jnp.float32).astype(jnp.bfloat16)
    grad_rows = (
        jnp.dot(picker, out_grad, preferred_element_type=jnp.float32) * slot_weight[:, None]
    ).astype(jnp.bfloat16)
    stacked = jnp.stack([x_rows, grad_rows])
    outgoing = jnp.broadcast_to(
        stacked.reshape(2, in_flight, 1, CAP, features), (2, in_flight, GROUP, CAP, features)
    )
    outgoing = outgoing.reshape(2, axis_width, CAP, features)
    arrived = lax.all_to_all(outgoing, "expert", split_axis=1, concat_axis=1, tiled=True)
    arrived = arrived.reshape(2, axis_width * CAP, features)
    row_grad, grads = expert_backward(arrived[0], arrived[1], w_gate[0], w_up[0], w_down[0])
    returned = lax.all_to_all(
        row_grad.reshape(axis_width, CAP, features),
        "expert",
        split_axis=0,
        concat_axis=0,
        tiled=True,
    )
    summed = jnp.sum(returned.reshape(in_flight, GROUP, CAP, features), axis=1).reshape(
        in_flight * CAP, features
    )
    tokens_grad = lax.dot_general(
        select,
        summed,
        (((0,), (0,)), ((), ())),
        precision=lax.Precision.HIGHEST,
        preferred_element_type=jnp.float32,
    )
    tokens_grad = tokens_grad.astype(jnp.bfloat16)
    half_rows = features // 2
    section_count = lax.axis_size("pipe")
    section_bits = section_count.bit_length() - 1
    lower_section = lax.axis_index("pipe") < section_count // 2
    retained_grads = jnp.where(lower_section, grads[:, :half_rows], grads[:, half_rows:])
    incoming = jnp.where(lower_section, grads[:, half_rows:], grads[:, :half_rows])
    for level in range(section_bits):
        incoming = from_partner(incoming, "pipe", level)
    weight_grads = (retained_grads.astype(jnp.float32) + incoming.astype(jnp.float32)).astype(
        jnp.bfloat16
    )
    return (tokens_grad, weight_grads[None])


def solution(mesh):
    return jax.shard_map(
        body,
        mesh=mesh,
        in_specs=(
            P(("pipe", "expert"), None),
            P(("pipe", "expert"), None),
            P(("pipe", "expert"), None),
            P(("pipe", "expert"), None),
            P("pipe", None, "expert"),
            P("pipe", None, "expert"),
            P("pipe", "expert", None),
        ),
        out_specs=(P(("pipe", "expert"), None), P("pipe", None, None, "expert")),
        check_vma=False,
    )
```

profile of v0, /device:TPU:0, one launch (start us, length us, event | category | flops | bytes accessed | tf_op | source)
XLA Modules:
  0.0 215.8 jit_solution(13394034376812539002)
XLA Ops:
  0.6 0.0 copy-start
  0.6 0.9 select_reduce_fusion
  1.5 0.1 copy.11
  1.6 0.2 reduce-window.7
  1.8 0.1 reduce.6
  1.9 0.1 convolution_bitcast_fusion
  2.1 1.4 fusion.5
  3.5 1.4 fusion.6
  4.9 1.0 reshape.147
  5.9 5.2 %all-to-all-start = ((bf16[2,8,8,3584]{3,2,0,1:T(8,128)(2,1)}), bf16[2,8,8,3584]{3,2,0,1:T(8,128)(2,1)S(1)}, u32[]{:S(2)}, u32[]{:S(2)}) async-start(bf16[2,8,8,3584]{3,2,0,1:T(8,128)(2,1)} %reshape.147), calls=%async_computation | async-start | bytes 1835008 | tf_op jit(solution)/shard_map/all_to_all | solution.py:72
  11.1 14.0 %all-to-all-done = bf16[2,8,8,3584]{3,2,0,1:T(8,128)(2,1)S(1)} async-done(((bf16[2,8,8,3584]{3,2,0,1:T(8,128)(2,1)}), bf16[2,8,8,3584]{3,2,0,1:T(8,128)(2,1)S(1)}, u32[]{:S(2)}, u32[]{:S(2)}) %all-to-all-start) | async-done | bytes 917536 | tf_op jit(solution)/shard_map/all_to_all | solution.py:72
  25.1 0.0 copy-done
  25.1 0.0 copy-start.2
  25.1 0.4 fusion.10
  25.5 1.1 copy-done.2
  26.6 0.0 copy-start.3
  26.6 0.4 fusion.13
  27.0 0.7 fusion.2
  27.7 0.4 copy-done.3
  28.1 0.7 multiply_convert_fusion.1
  28.8 0.7 fusion
  29.4 0.7 fusion.1
  30.1 0.7 pad_maximum_fusion
  30.8 0.0 copy-start.1
  30.8 0.3 broadcast_select_fusion
  31.1 2.1 copy-done.1
  33.2 1.6 collective-permute-start
  34.8 57.2 %collective-permute-done = bf16[3,1792,256]{2,1,0:T(8,128)(2,1)} collective-permute-done((bf16[3,1792,256]{2,1,0:T(8,128)(2,1)S(1)}, bf16[3,1792,256]{2,1,0:T(8,128)(2,1)}, u32[]{:S(2)}, u32[]{:S(2)}) %collective-permute-start) | collective-permute-done | bytes 2752544 | tf_op jit(solution)/shard_map/ppermute | solution.py:13
  91.9 3.6 %collective-permute-start.1 = (bf16[3,1792,256]{2,1,0:T(8,128)(2,1)}, bf16[3,1792,256]{2,1,0:T(8,128)(2,1)}, u32[]{:S(2)}, u32[]{:S(2)}) collective-permute-start(bf16[3,1792,256]{2,1,0:T(8,128)(2,1)} %collective-permute-done), channel_id=1, source_target_pairs={{0,16},{8,24},{16,0},{24,8},{1,17},{9,25},{17,1},{25,9},{2,18},{10... | collective-permute-start | bytes 8257544 | tf_op jit(solution)/shard_map/ppermute | solution.py:13
  95.5 0.7 fusion.8
  96.2 0.7 fusion.3
  96.9 17.6 %all_to_all.10 = f32[8,8,3584]{2,1,0:T(8,128)S(1)} all-to-all(f32[8,8,3584]{2,1,0:T(8,128)S(1)} %fusion.3), channel_id=1, replica_groups=mesh['pipe'=4,'expert'=8] {'expert'}, dimensions={0} | all-to-all | bytes 1835008 | tf_op jit(solution)/shard_map/all_to_all | solution.py:75
  114.5 1.9 convolution_convert_fusion.3
  116.3 93.5 %collective-permute-done.1 = bf16[3,1792,256]{2,1,0:T(8,128)(2,1)} collective-permute-done((bf16[3,1792,256]{2,1,0:T(8,128)(2,1)}, bf16[3,1792,256]{2,1,0:T(8,128)(2,1)}, u32[]{:S(2)}, u32[]{:S(2)}) %collective-permute-start.1) | collective-permute-done | bytes 2752544 | tf_op jit(solution)/shard_map/ppermute | solution.py:13
  209.9 6.0 %fusion.7 = bf16[1,3,1792,256]{3,2,1,0:T(8,128)(2,1)} fusion(bf16[3,1792,256]{2,1,0:T(8,128)(2,1)} %collective-permute-done.1, pred[]{:T(512)S(6)} %lt.3, bf16[3,3584,256]{2,1,0:T(8,128)(2,1)} %copy-done.1), kind=kLoop, calls=%fused_computation.16 | loop fusion | flops 6881280 | bytes 11010049 | tf_op jit(solution)/shard_map/broadcast_in_dim | solution.py:104
  (5 shorter events, 0.1 us)
Async XLA Ops:
  0.6 24.4 %copy-start = (bf16[1,3584,256]{2,1,0:T(8,128)(2,1)S(1)}, bf16[1,3584,256]{2,1,0:T(8,128)(2,1)}, u32[]{:S(2)}) copy-start(bf16[1,3584,256]{2,1,0:T(8,128)(2,1)} %param.11) | copy-start | bytes 5505028
  5.9 19.2 %all-to-all-start = ((bf16[2,8,8,3584]{3,2,0,1:T(8,128)(2,1)}), bf16[2,8,8,3584]{3,2,0,1:T(8,128)(2,1)S(1)}, u32[]{:S(2)}, u32[]{:S(2)}) async-start(bf16[2,8,8,3584]{3,2,0,1:T(8,128)(2,1)} %reshape.147), calls=%async_computation | async-start | bytes 1835008 | tf_op jit(solution)/shard_map/all_to_all | solution.py:72
  25.1 1.5 copy-start.2
  26.6 1.5 copy-start.3
  30.8 2.4 %copy-start.1 = (bf16[3,3584,256]{2,1,0:T(8,128)(2,1)}, bf16[3,3584,256]{2,1,0:T(8,128)(2,1)S(1)}, u32[]{:S(2)}) copy-start(bf16[3,3584,256]{2,1,0:T(8,128)(2,1)S(1)} %pad_maximum_fusion) | copy-start | bytes 16515076
  33.2 58.8 %collective-permute-start = (bf16[3,1792,256]{2,1,0:T(8,128)(2,1)S(1)}, bf16[3,1792,256]{2,1,0:T(8,128)(2,1)}, u32[]{:S(2)}, u32[]{:S(2)}) collective-permute-start(bf16[3,1792,256]{2,1,0:T(8,128)(2,1)S(1)} %broadcast_select_fusion), channel_id=1, source_target_pairs={{0,8},{8,0},{16,24},{24,16},{1,9},{9,1},{17,25},{25,17},{2,10},{10... | collective-permute-start | bytes 8257544 | tf_op jit(solution)/shard_map/ppermute | solution.py:13
  91.9 117.9 %collective-permute-start.1 = (bf16[3,1792,256]{2,1,0:T(8,128)(2,1)}, bf16[3,1792,256]{2,1,0:T(8,128)(2,1)}, u32[]{:S(2)}, u32[]{:S(2)}) collective-permute-start(bf16[3,1792,256]{2,1,0:T(8,128)(2,1)} %collective-permute-done), channel_id=1, source_target_pairs={{0,16},{8,24},{16,0},{24,8},{1,17},{9,25},{17,1},{25,9},{2,18},{10... | collective-permute-start | bytes 8257544 | tf_op jit(solution)/shard_map/ppermute | solution.py:13
where the time goes:
time: 220 us; the launch traced here: 216 us
  waiting for transfers between devices  165 us (75%)
  blocking collectives  17.6 us (8%)
  starting transfers between devices  10.3 us (5%)
  matrix products  9.7 us (4%)
  other arithmetic  8.15 us (4%)
  local copies, waits for them, and re-layouts  4.65 us (2%)
    ppermute x2, waiting for transfers between devices, from_partner(): return lax.ppermute(value, axis, pairs)  151 us
    all_to_all x1, blocking collectives, body(): lax.all_to_all(row_grad.reshape(axis_width, CAP, features), 'expert', spl...  17.6 us
    all_to_all x1, waiting for transfers between devices, body(): lax.all_to_all(outgoing, 'expert', split_axis=1, concat_axis=1, tiled=True)  14 us
    broadcast_in_dim x1, other arithmetic, body(): return (tokens_grad, weight_grads[None])  5.96 us
    all_to_all x1, starting transfers between devices, body(): lax.all_to_all(outgoing, 'expert', split_axis=1, concat_axis=1, tiled=True)  5.17 us
    ppermute x2, starting transfers between devices, from_partner(): return lax.ppermute(value, axis, pairs)  5.17 us
  transfers between devices with their start and end apart: 3, of which 3 were waited for; matrix products, arithmetic and copies ran while one was open for 2% of the time, Pallas kernels for 0%

commit v1 on v0

--- a/solution.py
+++ b/solution.py
@@ -5,12 +5,6 @@
 
 GROUP = 8
 CAP = 8
-
-
-def from_partner(value, axis, apart):
-    mask = 2**apart
-    pairs = [(source, source ^ mask) for source in range(lax.axis_size(axis))]
-    return lax.ppermute(value, axis, pairs)
 
 
 def route_slots(block_ids, block_probs, in_flight):
@@ -34,7 +28,12 @@
     )
 
 
-def expert_backward(x_rows, grad_rows, gate_cols, up_cols, down_rows):
+def to_mirror(value):
+    count = lax.axis_size("pipe")
+    return lax.ppermute(value, "pipe", [(k, count - 1 - k) for k in range(count)])
+
+
+def expert_activations(x_rows, grad_rows, gate_cols, up_cols, down_rows):
     gate = jnp.dot(x_rows, gate_cols, preferred_element_type=jnp.float32)
     up = jnp.dot(x_rows, up_cols, preferred_element_type=jnp.float32)
     sigmoid_gate = jax.nn.sigmoid(gate)
@@ -43,21 +42,15 @@
     back = contract(grad_rows, down_rows, 1, 1)
     d_gate = (back * up * sigmoid_gate * (1.0 + gate * (1.0 - sigmoid_gate))).astype(jnp.bfloat16)
     d_up = (back * activated).astype(jnp.bfloat16)
-    row_grad = contract(d_gate, gate_cols, 1, 1) + contract(d_up, up_cols, 1, 1)
-    grads = jnp.stack(
-        [
-            contract(x_rows, d_gate, 0, 0),
-            contract(x_rows, d_up, 0, 0),
-            contract(grad_rows, hidden, 0, 0),
-        ]
-    ).astype(jnp.bfloat16)
-    return (row_grad, grads)
+    return d_gate, d_up, hidden
 
 
 def body(tokens, out_grad, probs, expert_ids, w_gate, w_up, w_down):
     axis_width = lax.axis_size("expert")
     in_flight = axis_width // GROUP
     features = tokens.shape[1]
+    half = features // 2
+    lower = lax.axis_index("pipe") < lax.axis_size("pipe") // 2
     select, slot_weight = route_slots(expert_ids, probs, in_flight)
     picker = select.astype(jnp.bfloat16)
     x_rows = jnp.dot(picker, tokens, preferred_element_type=jnp.float32).astype(jnp.bfloat16)
@@ -65,13 +58,23 @@
         jnp.dot(picker, out_grad, preferred_element_type=jnp.float32) * slot_weight[:, None]
     ).astype(jnp.bfloat16)
     stacked = jnp.stack([x_rows, grad_rows])
-    outgoing = jnp.broadcast_to(
-        stacked.reshape(2, in_flight, 1, CAP, features), (2, in_flight, GROUP, CAP, features)
+    mirrored = to_mirror(jnp.where(lower, stacked[:, :, half:], stacked[:, :, :half]))
+
+    def spread(rows):
+        width = rows.shape[-1]
+        rows = jnp.broadcast_to(
+            rows.reshape(2, in_flight, 1, CAP, width), (2, in_flight, GROUP, CAP, width)
+        ).reshape(2, axis_width, CAP, width)
+        rows = lax.all_to_all(rows, "expert", split_axis=1, concat_axis=1, tiled=True)
+        return rows.reshape(2, axis_width * CAP, width)
+
+    arrived = spread(stacked)
+    d_gate, d_up, hidden = expert_activations(
+        arrived[0], arrived[1], w_gate[0], w_up[0], w_down[0]
     )
-    outgoing = outgoing.reshape(2, axis_width, CAP, features)
-    arrived = lax.all_to_all(outgoing, "expert", split_axis=1, concat_axis=1, tiled=True)
-    arrived = arrived.reshape(2, axis_width * CAP, features)
-    row_grad, grads = expert_backward(arrived[0], arrived[1], w_gate[0], w_up[0], w_down[0])
+    activations = jnp.stack([d_gate, d_up, hidden])
+    other_activations = to_mirror(activations)
+    row_grad = contract(d_gate, w_gate[0], 1, 1) + contract(d_up, w_up[0], 1, 1)
     returned = lax.all_to_all(
         row_grad.reshape(axis_width, CAP, features),
         "expert",
@@ -90,17 +93,17 @@
         preferred_element_type=jnp.float32,
     )
     tokens_grad = tokens_grad.astype(jnp.bfloat16)
-    half_rows = features // 2
-    section_count = lax.axis_size("pipe")
-    section_bits = section_count.bit_length() - 1
-    lower_section = lax.axis_index("pipe") < section_count // 2
-    retained_grads = jnp.where(lower_section, grads[:, :half_rows], grads[:, half_rows:])
-    incoming = jnp.where(lower_section, grads[:, half_rows:], grads[:, :half_rows])
-    for level in range(section_bits):
-        incoming = from_partner(incoming, "pipe", level)
-    weight_grads = (retained_grads.astype(jnp.float32) + incoming.astype(jnp.float32)).astype(
-        jnp.bfloat16
-    )
+    other = spread(mirrored)
+    kept = jnp.where(lower, arrived[:, :, :half], arrived[:, :, half:])
+    rows = jnp.concatenate([kept, other], axis=1)
+    right = jnp.concatenate([activations, other_activations], axis=1)
+    weight_grads = jnp.stack(
+        [
+            contract(rows[0], right[0], 0, 0),
+            contract(rows[0], right[1], 0, 0),
+            contract(rows[1], right[2], 0, 0),
+        ]
+    ).astype(jnp.bfloat16)
     return (tokens_grad, weight_grads[None])
 
 

time: 220 us -> 75.7 us (0.34); the launches traced: 216 us -> 75.2 us
  waiting for transfers between devices: 165 us -> 35 us
  blocking collectives: 17.6 us -> 0 us
  starting transfers between devices: 10.3 us -> 20.6 us
  other arithmetic: 8.15 us -> 5.11 us
    ppermute x2, waiting for transfers between devices: 151 us -> 2.22 us  [to_mirror(): lax.ppermute(value, 'pipe', [(k, count - 1 - k) for k in range(count)])]
    all_to_all x1 -> x3, waiting for transfers between devices: 14 us -> 32.7 us  [the longest x2 21.9 us: spread(): lax.all_to_all(rows, 'expert', split_axis=1, concat_axis=1, tiled=True)]
    all_to_all x1 -> x0, blocking collectives: 17.6 us -> none  [body(): lax.all_to_all(row_grad.reshape(axis_width, CAP, features), 'expert', spl...]
    all_to_all x1 -> x3, starting transfers between devices: 5.17 us -> 11.8 us  [the longest x2 7.5 us: spread(): lax.all_to_all(rows, 'expert', split_axis=1, concat_axis=1, tiled=True)]
    broadcast_in_dim x1 -> x0, other arithmetic: 5.96 us -> none  [body(): return (tokens_grad, weight_grads[None])]
    ppermute x2, starting transfers between devices: 5.17 us -> 8.72 us  [to_mirror(): lax.ppermute(value, 'pipe', [(k, count - 1 - k) for k in range(count)])]
    unnamed x8 -> x10, local copies, waits for them, and re-layouts: 3.55 us -> 0.82 us
  transfers between devices with their start and end apart: 3 -> 5, of which waited for: 3 -> 4; matrix products, arithmetic and copies ran while one was open for 2% -> 8% of each run, Pallas kernels for 0% -> 0%
where the time goes in v1:
time: 75.7 us; the launch traced here: 75.2 us
  waiting for transfers between devices  35 us (46%)
  starting transfers between devices  20.6 us (27%)
  matrix products  9.87 us (13%)
  other arithmetic  5.11 us (7%)
  local copies, waits for them, and re-layouts  3.89 us (5%)
  between operations  0.77 us (1%)
    all_to_all x2, waiting for transfers between devices, spread(): lax.all_to_all(rows, 'expert', split_axis=1, concat_axis=1, tiled=True)  21.9 us
    all_to_all x1, waiting for transfers between devices, body(): lax.all_to_all(row_grad.reshape(axis_width, CAP, features), 'expert', spl...  10.8 us
    ppermute x2, starting transfers between devices, to_mirror(): lax.ppermute(value, 'pipe', [(k, count - 1 - k) for k in range(count)])  8.72 us
    all_to_all x2, starting transfers between devices, spread(): lax.all_to_all(rows, 'expert', split_axis=1, concat_axis=1, tiled=True)  7.5 us
    all_to_all x1, starting transfers between devices, body(): lax.all_to_all(row_grad.reshape(axis_width, CAP, features), 'expert', spl...  4.35 us
    dot_general x6, matrix products, contract(): lax.dot_general(left, right, (((left_dim,), (right_dim,)), ((), ())), pre...  4.22 us
    ppermute x2, waiting for transfers between devices, to_mirror(): lax.ppermute(value, 'pipe', [(k, count - 1 - k) for k in range(count)])  2.22 us
    dot_general x1, matrix products, body(): lax.dot_general(select, summed, (((0,), (0,)), ((), ())), precision=lax.P...  1.85 us
  transfers between devices with their start and end apart: 5, of which 4 were waited for; matrix products, arithmetic and copies ran while one was open for 8% of the time, Pallas kernels for 0%

profile of v1, /device:TPU:0, one launch (start us, length us, event | category | flops | bytes accessed | tf_op | source)
XLA Modules:
  0.0 75.2 jit_solution(11499607354051669386)
XLA Ops:
  0.6 0.0 copy-start
  0.6 0.9 %select_reduce_fusion = (f32[128]{0:T(128)S(1)}, pred[128,8]{0,1:T(8,128)(4,1)S(1)}) fusion(bf16[128,8]{0,1:T(8,128)(2,1)} %param.9, s32[128,8]{0,1:T(8,128)} %param.10), kind=kLoop, calls=%fused_computation.56 | loop fusion | flops 3968 | bytes 7680 | tf_op jit(solution)/shard_map/reduce_sum | solution.py:14
  1.5 0.1 copy.12
  1.6 0.2 reduce-window.7
  1.8 0.1 reduce.6
  1.9 0.1 convolution_bitcast_fusion
  2.1 1.4 %fusion.2 = bf16[1,8,3584]{2,1,0:T(8,128)(2,1)S(1)} fusion(bf16[128,3584]{1,0:T(8,128)(2,1)} %param.7, s32[128]{0:T(128)S(1)} %convert_subtract_fusion, pred[128]{0:T(512)(128)(4,1)S(1)} %get-tuple-element.7), kind=kOutput, calls=%fused_computation.6 | convolution fusion | flops 7372800 | bytes 975488 | tf_op jit(solution)/shard_map/dot_general | solution.py:56
  3.5 1.4 %fusion.3 = bf16[1,8,3584]{2,1,0:T(8,128)(2,1)S(1)} fusion(bf16[128,3584]{1,0:T(8,128)(2,1)} %param.8, f32[8]{0:T(128)S(1)} %convolution_bitcast_fusion, s32[128]{0:T(128)S(1)} %convert_subtract_fusion, pred[128]{0:T(512)(128)(4,1)S(1)} %get-tuple-element.7), kind=kOutput, calls=%fused_computation.7 | convolution fusion | flops 7401472 | bytes 975520 | tf_op jit(solution)/shard_map/dot_general | solution.py:58
  4.9 5.1 %collective-permute-start = (bf16[2,8,1792]{2,1,0:T(8,128)(2,1)S(1)}, bf16[2,8,1792]{2,1,0:T(8,128)(2,1)S(1)}, u32[]{:S(2)}, u32[]{:S(2)}) collective-permute-start(bf16[2,8,1792]{2,1,0:T(8,128)(2,1)S(1)} %fusion.23), channel_id=1, source_target_pairs={{0,24},{8,16},{16,8},{24,0},{1,25},{9,17},{17,9},{25,1},{2,26},{10... | collective-permute-start | bytes 172040 | tf_op jit(solution)/shard_map/ppermute | solution.py:33
  10.0 2.2 %collective-permute-done = bf16[2,8,1792]{2,1,0:T(8,128)(2,1)S(1)} collective-permute-done((bf16[2,8,1792]{2,1,0:T(8,128)(2,1)S(1)}, bf16[2,8,1792]{2,1,0:T(8,128)(2,1)S(1)}, u32[]{:S(2)}, u32[]{:S(2)}) %collective-permute-start) | collective-permute-done | bytes 57376 | tf_op jit(solution)/shard_map/ppermute | solution.py:33
  12.2 0.8 %reshape.210 = bf16[2,8,8,1792]{3,2,0,1:T(8,128)(2,1)} broadcast(bf16[2,8,1792]{2,1,0:T(8,128)(2,1)S(1)} %collective-permute-done), dimensions={0,2,3} | broadcast | bytes 516096 | tf_op jit(solution)/shard_map/reshape | solution.py:67
  13.0 3.9 %all-to-all-start.2 = ((bf16[2,8,8,1792]{3,2,0,1:T(8,128)(2,1)}), bf16[2,8,8,1792]{3,2,0,1:T(8,128)(2,1)S(1)}, u32[]{:S(2)}, u32[]{:S(2)}) async-start(bf16[2,8,8,1792]{3,2,0,1:T(8,128)(2,1)} %reshape.210), calls=%async_computation.2 | async-start | bytes 917504 | tf_op jit(solution)/shard_map/all_to_all | solution.py:68
  17.0 9.0 %all-to-all-done.2 = bf16[2,8,8,1792]{3,2,0,1:T(8,128)(2,1)S(1)} async-done(((bf16[2,8,8,1792]{3,2,0,1:T(8,128)(2,1)}), bf16[2,8,8,1792]{3,2,0,1:T(8,128)(2,1)S(1)}, u32[]{:S(2)}, u32[]{:S(2)}) %all-to-all-start.2) | async-done | bytes 458784 | tf_op jit(solution)/shard_map/all_to_all | solution.py:68
  26.0 0.0 copy-start.4
  26.0 1.0 %reshape.207 = bf16[2,8,8,3584]{3,2,0,1:T(8,128)(2,1)} broadcast(bf16[2,8,3584]{2,1,0:T(8,128)(2,1)S(1)} %pad_maximum_fusion.3), dimensions={0,2,3} | broadcast | bytes 1032192 | tf_op jit(solution)/shard_map/reshape | solution.py:67
  27.1 0.0 copy-done.4
  27.1 3.6 %all-to-all-start = ((bf16[2,8,8,3584]{3,2,0,1:T(8,128)(2,1)}), bf16[2,8,8,3584]{3,2,0,1:T(8,128)(2,1)S(1)}, u32[]{:S(2)}, u32[]{:S(2)}) async-start(bf16[2,8,8,3584]{3,2,0,1:T(8,128)(2,1)} %reshape.207), calls=%async_computation | async-start | bytes 1835008 | tf_op jit(solution)/shard_map/all_to_all | solution.py:68
  30.7 1.1 %copy.18 = bf16[2,8,8,1792]{3,2,1,0:T(8,128)(2,1)S(1)} copy(bf16[2,8,8,1792]{3,2,0,1:T(8,128)(2,1)} %copy-done.4) | data formatting | bytes 917504 | tf_op jit(solution)/shard_map/all_to_all | solution.py:68
  31.7 12.9 %all-to-all-done = bf16[2,8,8,3584]{3,2,0,1:T(8,128)(2,1)S(1)} async-done(((bf16[2,8,8,3584]{3,2,0,1:T(8,128)(2,1)}), bf16[2,8,8,3584]{3,2,0,1:T(8,128)(2,1)S(1)}, u32[]{:S(2)}, u32[]{:S(2)}) %all-to-all-start) | async-done | bytes 917536 | tf_op jit(solution)/shard_map/all_to_all | solution.py:68
  44.6 0.1 copy.17
  44.7 0.0 copy-start.1
  44.7 0.8 %slice_select_fusion = bf16[2,64,1792]{2,1,0:T(8,128)(2,1)} fusion(bf16[2,64,3584]{2,1,0:T(8,128)(2,1)S(1)} %bitcast.77, pred[]{:T(512)S(6)} %lt.3), kind=kLoop, calls=%fused_computation.33 | loop fusion | flops 229376 | bytes 1376257 | tf_op jit(solution)/shard_map/jit(_where)/select_n | solution.py:97
  45.5 0.0 copy-done
  45.5 0.0 copy-start.3
  45.5 0.4 fusion.9
  45.9 0.4 copy-done.1
  46.3 0.4 fusion.12
  46.8 0.4 copy-done.3
  47.1 0.7 fusion.25
  47.8 0.7 fusion.7
  48.5 3.6 %collective-permute-start.1 = (bf16[3,64,256]{2,1,0:T(8,128)(2,1)S(1)}, bf16[3,64,256]{2,1,0:T(8,128)(2,1)S(1)}, u32[]{:S(2)}, u32[]{:S(2)}) collective-permute-start(bf16[3,64,256]{2,1,0:T(8,128)(2,1)S(1)} %pad_maximum_fusion.4), channel_id=1, source_target_pairs={{0,24},{8,16},{16,8},{24,0},{1,25},{9,17},{17,9},{25,1},{2,26},{10... | collective-permute-start | bytes 294920 | tf_op jit(solution)/shard_map/ppermute | solution.py:33
  52.1 1.6 %fusion = f32[8,8,3584]{2,1,0:T(8,128)} fusion(f32[64,3584]{1,0:T(8,128)S(1)} %fusion.7, bf16[64,256]{1,0:T(8,128)(2,1)S(1)} %get-tuple-element.6, bf16[1,3584,256]{2,1,0:T(8,128)(2,1)S(1)} %copy-done.1), kind=kOutput, calls=%fused_computation.2 | convolution fusion | flops 117669888 | bytes 3702784 | tf_op jit(solution)/shard_map/dot_general | solution.py:26
  53.7 0.0 copy-start.2
  53.7 4.3 %all-to-all-start.1 = ((f32[8,8,3584]{2,1,0:T(8,128)}), f32[8,8,3584]{2,1,0:T(8,128)}, u32[]{:S(2)}, u32[]{:S(2)}) async-start(f32[8,8,3584]{2,1,0:T(8,128)} %fusion), calls=%async_computation.1 | async-start | bytes 1835008 | tf_op jit(solution)/shard_map/all_to_all | solution.py:78
  58.1 0.0 collective-permute-done.1
  58.1 0.0 copy-done.2
  58.1 0.4 fusion.6
  58.5 0.4 fusion.5
  59.0 0.4 fusion.4
  59.4 1.8 %pad_maximum_fusion = bf16[1,3,1792,256]{3,2,1,0:T(8,128)(2,1)} fusion(bf16[1,1,1792,256]{3,2,1,0:T(8,128)(2,1)S(1)} %fusion.6, bf16[1,1,1792,256]{3,2,1,0:T(8,128)(2,1)S(1)} %fusion.5, bf16[1,1,1792,256]{3,2,1,0:T(8,128)(2,1)S(1)} %fusion.4), kind=kLoop, calls=%fused_computation.8 | loop fusion | flops 2752512 | bytes 5505024 | tf_op jit(solution)/shard_map/stack | solution.py:100
  61.2 10.8 %all-to-all-done.1 = f32[8,8,3584]{2,1,0:T(8,128)} async-done(((f32[8,8,3584]{2,1,0:T(8,128)}), f32[8,8,3584]{2,1,0:T(8,128)}, u32[]{:S(2)}, u32[]{:S(2)}) %all-to-all-start.1) | async-done | bytes 917536 | tf_op jit(solution)/shard_map/all_to_all | solution.py:78
  72.1 1.2 %reduce_sum.19 = f32[8,3584]{1,0:T(8,128)S(1)} reduce(f32[8,8,3584]{2,1,0:T(8,128)} %all-to-all-done.1, f32[]{:T(128)} %constant.5.clone.1), dimensions={0}, to_apply=%region_3.4 | reduce | flops 200704 | bytes 1032196 | tf_op jit(solution)/shard_map/reduce_sum | solution.py:85
  73.3 1.8 %convolution_convert_fusion = bf16[128,3584]{1,0:T(8,128)(2,1)} fusion(f32[8,3584]{1,0:T(8,128)S(1)} %reduce_sum.19, s32[128]{0:T(128)S(1)} %convert_subtract_fusion, pred[128]{0:T(512)(128)(4,1)S(1)} %get-tuple-element.7), kind=kOutput, calls=%fused_computation | convolution fusion | flops 44500992 | bytes 1032832 | tf_op jit(solution)/shard_map/dot_general | solution.py:88
  (7 shorter events, 0.1 us)
Async XLA Ops:
  0.6 44.9 %copy-start = (bf16[1,3584,256]{2,1,0:T(8,128)(2,1)S(1)}, bf16[1,3584,256]{2,1,0:T(8,128)(2,1)}, u32[]{:S(2)}) copy-start(bf16[1,3584,256]{2,1,0:T(8,128)(2,1)} %param.11) | copy-start | bytes 5505028
  4.9 7.3 %collective-permute-start = (bf16[2,8,1792]{2,1,0:T(8,128)(2,1)S(1)}, bf16[2,8,1792]{2,1,0:T(8,128)(2,1)S(1)}, u32[]{:S(2)}, u32[]{:S(2)}) collective-permute-start(bf16[2,8,1792]{2,1,0:T(8,128)(2,1)S(1)} %fusion.23), channel_id=1, source_target_pairs={{0,24},{8,16},{16,8},{24,0},{1,25},{9,17},{17,9},{25,1},{2,26},{10... | collective-permute-start | bytes 172040 | tf_op jit(solution)/shard_map/ppermute | solution.py:33
  13.0 13.0 %all-to-all-start.2 = ((bf16[2,8,8,1792]{3,2,0,1:T(8,128)(2,1)}), bf16[2,8,8,1792]{3,2,0,1:T(8,128)(2,1)S(1)}, u32[]{:S(2)}, u32[]{:S(2)}) async-start(bf16[2,8,8,1792]{3,2,0,1:T(8,128)(2,1)} %reshape.210), calls=%async_computation.2 | async-start | bytes 917504 | tf_op jit(solution)/shard_map/all_to_all | solution.py:68
  26.0 1.1 %copy-start.4 = (bf16[2,8,8,1792]{3,2,0,1:T(8,128)(2,1)}, bf16[2,8,8,1792]{3,2,0,1:T(8,128)(2,1)S(1)}, u32[]{:S(2)}) copy-start(bf16[2,8,8,1792]{3,2,0,1:T(8,128)(2,1)S(1)} %all-to-all-done.2) | copy-start | bytes 1376260
  27.1 17.5 %all-to-all-start = ((bf16[2,8,8,3584]{3,2,0,1:T(8,128)(2,1)}), bf16[2,8,8,3584]{3,2,0,1:T(8,128)(2,1)S(1)}, u32[]{:S(2)}, u32[]{:S(2)}) async-start(bf16[2,8,8,3584]{3,2,0,1:T(8,128)(2,1)} %reshape.207), calls=%async_computation | async-start | bytes 1835008 | tf_op jit(solution)/shard_map/all_to_all | solution.py:68
  44.7 1.7 %copy-start.1 = (bf16[1,3584,256]{2,1,0:T(8,128)(2,1)S(1)}, bf16[1,3584,256]{2,1,0:T(8,128)(2,1)}, u32[]{:S(2)}) copy-start(bf16[1,3584,256]{2,1,0:T(8,128)(2,1)} %param.12) | copy-start | bytes 5505028
  45.5 1.6 %copy-start.3 = (bf16[1,256,3584]{2,1,0:T(8,128)(2,1)S(1)}, bf16[1,256,3584]{2,1,0:T(8,128)(2,1)}, u32[]{:S(2)}) copy-start(bf16[1,256,3584]{2,1,0:T(8,128)(2,1)} %param.13) | copy-start | bytes 5505028
  48.5 9.6 %collective-permute-start.1 = (bf16[3,64,256]{2,1,0:T(8,128)(2,1)S(1)}, bf16[3,64,256]{2,1,0:T(8,128)(2,1)S(1)}, u32[]{:S(2)}, u32[]{:S(2)}) collective-permute-start(bf16[3,64,256]{2,1,0:T(8,128)(2,1)S(1)} %pad_maximum_fusion.4), channel_id=1, source_target_pairs={{0,24},{8,16},{16,8},{24,0},{1,25},{9,17},{17,9},{25,1},{2,26},{10... | collective-permute-start | bytes 294920 | tf_op jit(solution)/shard_map/ppermute | solution.py:33
  53.7 4.4 %copy-start.2 = (bf16[2,64,1792]{2,1,0:T(8,128)(2,1)S(1)}, bf16[2,64,1792]{2,1,0:T(8,128)(2,1)}, u32[]{:S(2)}) copy-start(bf16[2,64,1792]{2,1,0:T(8,128)(2,1)} %slice_select_fusion) | copy-start | bytes 1376260
  53.7 18.4 %all-to-all-start.1 = ((f32[8,8,3584]{2,1,0:T(8,128)}), f32[8,8,3584]{2,1,0:T(8,128)}, u32[]{:S(2)}, u32[]{:S(2)}) async-start(f32[8,8,3584]{2,1,0:T(8,128)} %fusion), calls=%async_computation.1 | async-start | bytes 1835008 | tf_op jit(solution)/shard_map/all_to_all | solution.py:78

commit v2 on v1

--- a/solution.py
+++ b/solution.py
@@ -1,10 +1,14 @@
 import jax
 import jax.numpy as jnp
 from jax import lax
+from jax.experimental import pallas as pl
+from jax.experimental.pallas import tpu as pltpu
 from jax.sharding import PartitionSpec as P
 
 GROUP = 8
 CAP = 8
+MESH = pl.DeviceIdType.MESH
+TILE = 256
 
 
 def route_slots(block_ids, block_probs, in_flight):
@@ -107,9 +111,216 @@
     return (tokens_grad, weight_grads[None])
 
 
+def exchange_kernel(
+    own, wg_hbm, wu_hbm, wd_hbm,
+    rows_out, acts_out, summed_out,
+    wg, wu, wd, rows, half_rows, mirror_rows, acts, other_acts, parts, returned,
+    load_sem, row_send, row_recv, half_send, half_recv, mirror_send, mirror_recv,
+    acts_send, acts_recv, part_send, part_recv,
+):
+    group = rows.shape[0]
+    features = own.shape[1]
+    half = features // 2
+    me = lax.axis_index("expert")
+    section = lax.axis_index("pipe")
+    sections = lax.axis_size("pipe")
+    opposite = sections - 1 - section
+    kept = pl.multiple_of(half * (section // (sections // 2)), 128)
+    sent = pl.multiple_of(half - kept, 128)
+
+    loads = [
+        pltpu.make_async_copy(source.at[0], target, load_sem.at[i])
+        for i, (source, target) in enumerate(((wg_hbm, wg), (wu_hbm, wu), (wd_hbm, wd)))
+    ]
+    for load in loads:
+        load.start()
+
+    def peer(step):
+        return lax.rem(me + step, group)
+
+    def from_peer(step):
+        return lax.rem(me + group - step, group)
+
+    def to_peers(source, target, send, recv):
+        return [
+            pltpu.make_async_remote_copy(
+                src_ref=source(peer(step)), dst_ref=target.at[me],
+                send_sem=send.at[step], recv_sem=recv.at[step],
+                device_id={"expert": peer(step)}, device_id_type=MESH,
+            )
+            for step in range(1, group)
+        ]
+
+    def arrivals(target, send, recv):
+        for step in range(1, group):
+            source = from_peer(step)
+            pltpu.make_async_remote_copy(
+                src_ref=target.at[source], dst_ref=target.at[source],
+                send_sem=send.at[step], recv_sem=recv.at[step],
+                device_id={"expert": source}, device_id_type=MESH,
+            ).wait_recv()
+
+    barrier = pltpu.get_barrier_semaphore()
+    for step in range(1, group):
+        pl.semaphore_signal(
+            barrier, inc=1, device_id={"expert": peer(step)}, device_id_type=MESH
+        )
+    pl.semaphore_signal(barrier, inc=1, device_id={"pipe": opposite}, device_id_type=MESH)
+    pl.semaphore_wait(barrier, group)
+
+    half_copy = pltpu.make_async_remote_copy(
+        src_ref=own.at[:, pl.ds(sent, half)], dst_ref=half_rows,
+        send_sem=half_send, recv_sem=half_recv,
+        device_id={"pipe": opposite}, device_id_type=MESH,
+    )
+    half_copy.start()
+    row_copies = to_peers(lambda _: own, rows, row_send, row_recv)
+    for copy in row_copies:
+        copy.start()
+    rows[me] = own[...]
+    half_copy.wait_recv()
+    mirror_copies = to_peers(lambda _: half_rows, mirror_rows, mirror_send, mirror_recv)
+    for copy in mirror_copies:
+        copy.start()
+    mirror_rows[me] = half_rows[...]
+    for load in loads:
+        load.wait()
+    arrivals(rows, row_send, row_recv)
+
+    both = rows[...].reshape(group * 2 * CAP, features)
+
+    def part_of(product, which):
+        split = product.reshape(group, 2 * CAP, product.shape[1])
+        return split[:, which * CAP : (which + 1) * CAP].reshape(group * CAP, -1)
+
+    gate = part_of(jnp.dot(both, wg[...], preferred_element_type=jnp.float32), 0)
+    up = part_of(jnp.dot(both, wu[...], preferred_element_type=jnp.float32), 0)
+    back = part_of(contract(both, wd[...], 1, 1), 1)
+    sigmoid_gate = jax.nn.sigmoid(gate)
+    activated = gate * sigmoid_gate
+    d_gate = (back * up * sigmoid_gate * (1.0 + gate * (1.0 - sigmoid_gate))).astype(jnp.bfloat16)
+    d_up = (back * activated).astype(jnp.bfloat16)
+    acts[0] = d_gate
+    acts[1] = d_up
+    acts[2] = (activated * up).astype(jnp.bfloat16)
+    acts_copy = pltpu.make_async_remote_copy(
+        src_ref=acts, dst_ref=other_acts,
+        send_sem=acts_send, recv_sem=acts_recv,
+        device_id={"pipe": opposite}, device_id_type=MESH,
+    )
+    acts_copy.start()
+
+    def row_grad(start):
+        columns = pl.ds(start, TILE)
+        tile = contract(d_gate, wg[columns, :], 1, 1) + contract(d_up, wu[columns, :], 1, 1)
+        return tile.reshape(group, CAP, TILE)
+
+    for start in range(0, half, TILE):
+        tile = jnp.concatenate([row_grad(start), row_grad(half + start)], axis=1)
+        parts[:, :, start : start + TILE] = tile.astype(jnp.bfloat16)
+    part_copies = to_peers(lambda index: parts.at[index], returned, part_send, part_recv)
+    for copy in part_copies:
+        copy.start()
+    returned[me] = parts[me]
+
+    rows_out[0:group] = rows[:, :, pl.ds(kept, half)]
+    acts_out[0] = acts[...]
+    arrivals(mirror_rows, mirror_send, mirror_recv)
+    rows_out[group : 2 * group] = mirror_rows[...]
+    acts_copy.wait_recv()
+    acts_out[1] = other_acts[...]
+    arrivals(returned, part_send, part_recv)
+    total = returned[0].astype(jnp.float32)
+    for index in range(1, group):
+        total = total + returned[index].astype(jnp.float32)
+    summed_out[...] = total
+    half_copy.wait_send()
+    acts_copy.wait_send()
+    for copy in row_copies + mirror_copies + part_copies:
+        copy.wait_send()
+
+
+def exchange(own, w_gate, w_up, w_down):
+    group = lax.axis_size("expert")
+    features = own.shape[1]
+    half = features // 2
+    hidden = w_gate.shape[2]
+    slots = group * CAP
+    vmem = pl.BlockSpec(memory_space=pltpu.VMEM)
+    anywhere = pl.BlockSpec(memory_space=pl.ANY)
+    bf16 = jnp.bfloat16
+    dma = pltpu.SemaphoreType.DMA
+    return pl.pallas_call(
+        exchange_kernel,
+        out_shape=(
+            jax.ShapeDtypeStruct((2 * group, 2 * CAP, half), bf16),
+            jax.ShapeDtypeStruct((2, 3, slots, hidden), bf16),
+            jax.ShapeDtypeStruct((2 * CAP, half), jnp.float32),
+        ),
+        in_specs=[vmem, anywhere, anywhere, anywhere],
+        out_specs=(vmem, vmem, vmem),
+        scratch_shapes=[
+            pltpu.VMEM((features, hidden), bf16),
+            pltpu.VMEM((features, hidden), bf16),
+            pltpu.VMEM((hidden, features), bf16),
+            pltpu.VMEM((group, 2 * CAP, features), bf16),
+            pltpu.VMEM((2 * CAP, half), bf16),
+            pltpu.VMEM((group, 2 * CAP, half), bf16),
+            pltpu.VMEM((3, slots, hidden), bf16),
+            pltpu.VMEM((3, slots, hidden), bf16),
+            pltpu.VMEM((group, 2 * CAP, half), bf16),
+            pltpu.VMEM((group, 2 * CAP, half), bf16),
+            dma((3,)),
+            dma((group,)),
+            dma((group,)),
+            dma,
+            dma,
+            dma((group,)),
+            dma((group,)),
+            dma,
+            dma,
+            dma((group,)),
+            dma((group,)),
+        ],
+        compiler_params=pltpu.CompilerParams(
+            collective_id=0, has_side_effects=True, vmem_limit_bytes=40 * 1024 * 1024
+        ),
+    )(own, w_gate, w_up, w_down)
+
+
+def kernel_body(tokens, out_grad, probs, expert_ids, w_gate, w_up, w_down):
+    half = tokens.shape[1] // 2
+    select, slot_weight = route_slots(expert_ids, probs, 1)
+    picker = select.astype(jnp.bfloat16)
+    x_rows = jnp.dot(picker, tokens, preferred_element_type=jnp.float32)
+    grad_rows = jnp.dot(picker, out_grad, preferred_element_type=jnp.float32)
+    own = jnp.concatenate([x_rows, grad_rows * slot_weight[:, None]]).astype(jnp.bfloat16)
+    rows, acts, summed = exchange(own, w_gate, w_up, w_down)
+    summed = jnp.concatenate([summed[:CAP], summed[CAP:]], axis=1)
+    tokens_grad = lax.dot_general(
+        select,
+        summed,
+        (((0,), (0,)), ((), ())),
+        precision=lax.Precision.HIGHEST,
+        preferred_element_type=jnp.float32,
+    ).astype(jnp.bfloat16)
+    x_all = rows[:, :CAP].reshape(-1, half)
+    grad_all = rows[:, CAP:].reshape(-1, half)
+    right = [acts[:, i].reshape(-1, acts.shape[3]) for i in range(3)]
+    weight_grads = jnp.stack(
+        [
+            contract(x_all, right[0], 0, 0),
+            contract(x_all, right[1], 0, 0),
+            contract(grad_all, right[2], 0, 0),
+        ]
+    ).astype(jnp.bfloat16)
+    return (tokens_grad, weight_grads[None])
+
+
 def solution(mesh):
+    single = mesh.shape["expert"] == GROUP
     return jax.shard_map(
-        body,
+        kernel_body if single else body,
         mesh=mesh,
         in_specs=(
             P(("pipe", "expert"), None),

time: 75.7 us -> 39.1 us (0.52)
  waiting for transfers between devices: 35 us -> 0 us
  Pallas kernels: 0 us -> 27.1 us
  starting transfers between devices: 20.6 us -> 0 us
  matrix products: 9.87 us -> 4.9 us
  other arithmetic: 5.11 us -> 3.04 us
    all_to_all x3 -> x0, waiting for transfers between devices: 32.7 us -> none  [the longest x2 21.9 us: spread(): lax.all_to_all(rows, 'expert', split_axis=1, concat_axis=1, tiled=True)]
    pallas_call x0 -> x1, Pallas kernels: none -> 27.1 us  [exchange(): pl.pallas_call(exchange_kernel, out_shape=(jax.ShapeDtypeStruct((2 * grou...]
    all_to_all x3 -> x0, starting transfers between devices: 11.8 us -> none  [the longest x2 7.5 us: spread(): lax.all_to_all(rows, 'expert', split_axis=1, concat_axis=1, tiled=True)]
    ppermute x2 -> x0, starting transfers between devices: 8.72 us -> none  [to_mirror(): lax.ppermute(value, 'pipe', [(k, count - 1 - k) for k in range(count)])]
    dot_general x6 -> x3, matrix products: 4.22 us -> 1.28 us  [contract(): lax.dot_general(left, right, (((left_dim,), (right_dim,)), ((), ())), pre...]
    ppermute x2 -> x0, waiting for transfers between devices: 2.22 us -> none  [to_mirror(): lax.ppermute(value, 'pipe', [(k, count - 1 - k) for k in range(count)])]
    unnamed x10 -> x8, local copies, waits for them, and re-layouts: 0.82 us -> 3.01 us
    dot_general x5 -> x3, matrix products: 5.52 us -> 3.49 us  [the longest x1 1.85 us: kernel_body(): lax.dot_general(select, summed, (((0,), (0,)), ((), ())), precision=lax.P...]
  transfers between devices with their start and end apart: 5 -> 0, of which waited for: 4 -> 0; matrix products, arithmetic and copies ran while one was open for 8% -> 0% of each run, Pallas kernels for 0% -> 0%
where the time goes in v2:
time: 39.1 us; the launch traced here: 38.9 us
  Pallas kernels  27.1 us (69%)
  matrix products  4.9 us (13%)
  local copies, waits for them, and re-layouts  3.14 us (8%)
  other arithmetic  3.04 us (8%)
  between operations  0.73 us (2%)
    pallas_call x1, Pallas kernels, exchange(): pl.pallas_call(exchange_kernel, out_shape=(jax.ShapeDtypeStruct((2 * grou...  27.1 us
    unnamed x8, local copies, waits for them, and re-layouts  3.01 us
    dot_general x1, matrix products, kernel_body(): lax.dot_general(select, summed, (((0,), (0,)), ((), ())), precision=lax.P...  1.85 us
    another operation x1, other arithmetic, kernel_body(): jnp.stack([contract(x_all, right[0], 0, 0), contract(x_all, right[1], 0,...  1.83 us
    dot_general x1, matrix products, kernel_body(): x_rows = jnp.dot(picker, tokens, preferred_element_type=jnp.float32)  1.4 us
    dot_general x3, matrix products, contract(): lax.dot_general(left, right, (((left_dim,), (right_dim,)), ((), ())), pre...  1.28 us
    reduce_sum x1, other arithmetic, route_slots(): jnp.sum(jnp.where(hits, block_probs.astype(jnp.float32)[:, :, None], jnp....  0.87 us

profile of v2, /device:TPU:0, one launch (start us, length us, event | category | flops | bytes accessed | tf_op | source)
XLA Modules:
  0.0 38.9 jit_solution(6515174473045147184)
XLA Ops:
  0.6 0.0 copy-start
  0.6 0.0 copy-start.1
  0.7 0.9 %select_reduce_fusion = (f32[128]{0:T(128)S(1)}, pred[128,8]{0,1:T(8,128)(4,1)S(1)}) fusion(bf16[128,8]{0,1:T(8,128)(2,1)} %param.9, s32[128,8]{0,1:T(8,128)} %param.10), kind=kLoop, calls=%fused_computation.22 | loop fusion | flops 3968 | bytes 7680 | tf_op jit(solution)/shard_map/reduce_sum | solution.py:18
  1.6 0.1 copy.10
  1.7 0.2 reduce-window.7
  1.8 0.1 reduce.4
  2.0 0.1 convolution_bitcast_fusion
  2.1 0.0 copy-done
  2.1 0.2 fusion
  2.3 1.4 %convolution_convert_fusion.1 = bf16[8,3584]{1,0:T(8,128)(2,1)S(1)} fusion(bf16[128,3584]{1,0:T(8,128)(2,1)} %param.7, s32[128]{0:T(128)S(1)} %convert_subtract_fusion, pred[128]{0:T(512)(128)(4,1)S(1)} %get-tuple-element.15), kind=kOutput, calls=%fused_computation.3 | convolution fusion | flops 7372800 | bytes 975488 | tf_op jit(solution)/shard_map/dot_general | solution.py:295
  3.8 0.0 copy-done.1
  3.8 0.0 copy-start.2
  3.8 1.5 %copy-done.2 = bf16[1,3584,256]{2,1,0:T(8,128)(2,1)S(1)} copy-done((bf16[1,3584,256]{2,1,0:T(8,128)(2,1)S(1)}, bf16[1,3584,256]{2,1,0:T(8,128)(2,1)}, u32[]{:S(2)}) %copy-start.2) | copy-done | bytes 1835032
  5.3 0.0 copy-start.3
  5.3 1.5 %copy-done.3 = bf16[1,256,3584]{2,1,0:T(8,128)(2,1)S(1)} copy-done((bf16[1,256,3584]{2,1,0:T(8,128)(2,1)S(1)}, bf16[1,256,3584]{2,1,0:T(8,128)(2,1)}, u32[]{:S(2)}) %copy-start.3) | copy-done | bytes 1835032
  6.8 27.1 %shard_map.86 = (bf16[16,16,1792]{2,1,0:T(8,128)(2,1)S(1)}, bf16[2,3,64,256]{3,2,1,0:T(8,128)(2,1)S(1)}, f32[16,1792]{1,0:T(8,128)S(1)}) custom-call(bf16[16,3584]{1,0:T(8,128)(2,1)S(1)} %pad_maximum_fusion.1.own, bf16[1,3584,256]{2,1,0:T(8,128)(2,1)S(1)} %copy-done.1, bf16[1,3584,256]{2,1,0:T(8,128)(2,1)S(1)} %copy-done.2, bf16[1,256,3584]{2,1,0:T(8,128)(2,1)S(1)} %copy-done.3), custom_call_target="tpu_custom_call" | custom-call | tf_op jit(solution)/shard_map/pallas_call | solution.py:253
  33.9 0.4 %fusion.1 = bf16[1,1,1792,256]{3,2,1,0:T(8,128)(2,1)S(1)} fusion(bf16[128,256]{1,0:T(8,128)(2,1)S(1)} %bitcast.31, bf16[16,16,1792]{2,1,0:T(8,128)(2,1)S(1)} %get-tuple-element.6), kind=kOutput, calls=%fused_computation.8 | convolution fusion | flops 117899264 | bytes 1441792 | tf_op jit(solution)/shard_map/dot_general | solution.py:30
  34.3 0.4 %fusion.2 = bf16[1,1,1792,256]{3,2,1,0:T(8,128)(2,1)S(1)} fusion(bf16[128,256]{1,0:T(8,128)(2,1)S(1)} %bitcast.30, bf16[16,16,1792]{2,1,0:T(8,128)(2,1)S(1)} %get-tuple-element.6), kind=kOutput, calls=%fused_computation.9 | convolution fusion | flops 117899264 | bytes 1441792 | tf_op jit(solution)/shard_map/dot_general | solution.py:30
  34.8 0.4 %fusion.3 = bf16[1,1,1792,256]{3,2,1,0:T(8,128)(2,1)S(1)} fusion(bf16[128,256]{1,0:T(8,128)(2,1)S(1)} %bitcast.29, bf16[16,16,1792]{2,1,0:T(8,128)(2,1)S(1)} %get-tuple-element.6), kind=kOutput, calls=%fused_computation.10 | convolution fusion | flops 117899264 | bytes 1441792 | tf_op jit(solution)/shard_map/dot_general | solution.py:30
  35.2 1.8 %pad_maximum_fusion = bf16[1,3,1792,256]{3,2,1,0:T(8,128)(2,1)} fusion(bf16[1,1,1792,256]{3,2,1,0:T(8,128)(2,1)S(1)} %fusion.3, bf16[1,1,1792,256]{3,2,1,0:T(8,128)(2,1)S(1)} %fusion.2, bf16[1,1,1792,256]{3,2,1,0:T(8,128)(2,1)S(1)} %fusion.1), kind=kLoop, calls=%fused_computation.4 | loop fusion | flops 2752512 | bytes 5505024 | tf_op jit(solution)/shard_map/stack | solution.py:310
  37.1 1.9 %convolution_convert_fusion = bf16[128,3584]{1,0:T(8,128)(2,1)} fusion(f32[8,1792]{1,0:T(8,128)S(1)} %get-tuple-element.14, f32[8,1792]{1,0:T(8,128)S(1)} %get-tuple-element.13, s32[128]{0:T(128)S(1)} %convert_subtract_fusion, pred[128]{0:T(512)(128)(4,1)S(1)} %get-tuple-element.15), kind=kOutput, calls=%fused_computation | convolution fusion | flops 44529664 | bytes 1032832 | tf_op jit(solution)/shard_map/dot_general | solution.py:300
  (6 shorter events, 0.1 us)
Async XLA Ops:
  0.6 1.5 %copy-start = (bf16[128,3584]{1,0:T(8,128)(2,1)S(1)}, bf16[128,3584]{1,0:T(8,128)(2,1)}, u32[]{:S(2)}) copy-start(bf16[128,3584]{1,0:T(8,128)(2,1)} %param.8) | copy-start | bytes 2752516
  0.6 3.1 %copy-start.1 = (bf16[1,3584,256]{2,1,0:T(8,128)(2,1)S(1)}, bf16[1,3584,256]{2,1,0:T(8,128)(2,1)}, u32[]{:S(2)}) copy-start(bf16[1,3584,256]{2,1,0:T(8,128)(2,1)} %wg_hbm.1) | copy-start | bytes 5505028
  3.8 1.5 %copy-start.2 = (bf16[1,3584,256]{2,1,0:T(8,128)(2,1)S(1)}, bf16[1,3584,256]{2,1,0:T(8,128)(2,1)}, u32[]{:S(2)}) copy-start(bf16[1,3584,256]{2,1,0:T(8,128)(2,1)} %wu_hbm.1) | copy-start | bytes 5505028
  5.3 1.5 %copy-start.3 = (bf16[1,256,3584]{2,1,0:T(8,128)(2,1)S(1)}, bf16[1,256,3584]{2,1,0:T(8,128)(2,1)}, u32[]{:S(2)}) copy-start(bf16[1,256,3584]{2,1,0:T(8,128)(2,1)} %wd_hbm.1) | copy-start | bytes 5505028

commit v3 on v2

--- a/solution.py
+++ b/solution.py
@@ -160,6 +160,42 @@
                 device_id={"expert": source}, device_id_type=MESH,
             ).wait_recv()
 
+    chips = group // 2
+    sibling = me + 1 - 2 * lax.rem(me, 2)
+
+    def share(source, target, send, recv, index, slot, device):
+        return pltpu.make_async_remote_copy(
+            src_ref=source, dst_ref=target.at[slot],
+            send_sem=send.at[index], recv_sem=recv.at[index],
+            device_id={"expert": device}, device_id_type=MESH,
+        )
+
+    def spread(source, target, send, recv):
+        copies = [
+            share(source, target, send, recv, chip, me, peer(2 * chip))
+            for chip in range(1, chips)
+        ]
+        copies.append(share(source, target, send, recv, 0, me, sibling))
+        for copy in copies:
+            copy.start()
+        return copies
+
+    def relay(target, send, recv):
+        copies = []
+        for chip in range(1, chips):
+            slot = from_peer(2 * chip)
+            share(target.at[slot], target, send, recv, chip, slot, slot).wait_recv()
+            copy = share(target.at[slot], target, send, recv, chips + chip, slot, sibling)
+            copy.start()
+            copies.append(copy)
+        return copies
+
+    def relayed(target, send, recv):
+        share(target.at[sibling], target, send, recv, 0, sibling, sibling).wait_recv()
+        for chip in range(1, chips):
+            slot = lax.rem(sibling + group - 2 * chip, group)
+            share(target.at[slot], target, send, recv, chips + chip, slot, sibling).wait_recv()
+
     barrier = pltpu.get_barrier_semaphore()
     for step in range(1, group):
         pl.semaphore_signal(
@@ -174,18 +210,15 @@
         device_id={"pipe": opposite}, device_id_type=MESH,
     )
     half_copy.start()
-    row_copies = to_peers(lambda _: own, rows, row_send, row_recv)
-    for copy in row_copies:
-        copy.start()
+    row_copies = spread(own, rows, row_send, row_recv)
     rows[me] = own[...]
     half_copy.wait_recv()
-    mirror_copies = to_peers(lambda _: half_rows, mirror_rows, mirror_send, mirror_recv)
-    for copy in mirror_copies:
-        copy.start()
+    mirror_copies = spread(half_rows, mirror_rows, mirror_send, mirror_recv)
     mirror_rows[me] = half_rows[...]
+    row_copies += relay(rows, row_send, row_recv)
     for load in loads:
         load.wait()
-    arrivals(rows, row_send, row_recv)
+    relayed(rows, row_send, row_recv)
 
     both = rows[...].reshape(group * 2 * CAP, features)
 
@@ -209,6 +242,7 @@
         device_id={"pipe": opposite}, device_id_type=MESH,
     )
     acts_copy.start()
+    mirror_copies += relay(mirror_rows, mirror_send, mirror_recv)
 
     def row_grad(start):
         columns = pl.ds(start, TILE)
@@ -225,7 +259,7 @@
 
     rows_out[0:group] = rows[:, :, pl.ds(kept, half)]
     acts_out[0] = acts[...]
-    arrivals(mirror_rows, mirror_send, mirror_recv)
+    relayed(mirror_rows, mirror_send, mirror_recv)
     rows_out[group : 2 * group] = mirror_rows[...]
     acts_copy.wait_recv()
     acts_out[1] = other_acts[...]
@@ -283,7 +317,7 @@
             dma((group,)),
         ],
         compiler_params=pltpu.CompilerParams(
-            collective_id=0, has_side_effects=True, vmem_limit_bytes=40 * 1024 * 1024
+            collective_id=0, has_side_effects=True, vmem_limit_bytes=58 * 1024 * 1024
         ),
     )(own, w_gate, w_up, w_down)
 
@@ -306,13 +340,10 @@
     ).astype(jnp.bfloat16)
     x_all = rows[:, :CAP].reshape(-1, half)
     grad_all = rows[:, CAP:].reshape(-1, half)
-    right = [acts[:, i].reshape(-1, acts.shape[3]) for i in range(3)]
-    weight_grads = jnp.stack(
-        [
-            contract(x_all, right[0], 0, 0),
-            contract(x_all, right[1], 0, 0),
-            contract(grad_all, right[2], 0, 0),
-        ]
+    left = jnp.stack([x_all, x_all, grad_all])
+    right = acts.transpose(1, 0, 2, 3).reshape(3, -1, acts.shape[3])
+    weight_grads = lax.dot_general(
+        left, right, (((1,), (1,)), ((0,), (0,))), preferred_element_type=jnp.float32
     ).astype(jnp.bfloat16)
     return (tokens_grad, weight_grads[None])
 

time: 39.1 us -> 36.6 us (0.936)
  other arithmetic: 3.04 us -> 1.78 us
  local copies, waits for them, and re-layouts: 3.14 us -> 1.93 us
  Pallas kernels: 27.1 us -> 25.9 us
  matrix products: 4.9 us -> 6.01 us
    unnamed x8 -> x6, local copies, waits for them, and re-layouts: 3.01 us -> 0.02 us
    another operation x3 -> x2, other arithmetic: 2.11 us -> 0.27 us  [the longest x1 1.83 us: kernel_body(): jnp.stack([contract(x_all, right[0], 0, 0), contract(x_all, right[1], 0,...]
    another operation x0 -> x3, local copies, waits for them, and re-layouts: none -> 1.77 us  [kernel_body(): left = jnp.stack([x_all, x_all, grad_all])]
    pallas_call x1, Pallas kernels: 27.1 us -> 25.9 us  [exchange(): pl.pallas_call(exchange_kernel, out_shape=(jax.ShapeDtypeStruct((2 * grou...]
    dot_general x3 -> x1, matrix products: 1.28 us -> 2.4 us  [kernel_body(): lax.dot_general(left, right, (((1,), (1,)), ((0,), (0,))), preferred_elem...]
    concatenate x1, other arithmetic: 0.02 us -> 0.67 us  [kernel_body(): jnp.concatenate([x_rows, grad_rows * slot_weight[:, None]])]
where the time goes in v3:
time: 36.6 us; the launch traced here: 36.3 us
  Pallas kernels  25.9 us (71%)
  matrix products  6.01 us (16%)
  local copies, waits for them, and re-layouts  1.93 us (5%)
  other arithmetic  1.78 us (5%)
  between operations  0.71 us (2%)
    pallas_call x1, Pallas kernels, exchange(): pl.pallas_call(exchange_kernel, out_shape=(jax.ShapeDtypeStruct((2 * grou...  25.9 us
    dot_general x1, matrix products, kernel_body(): lax.dot_general(left, right, (((1,), (1,)), ((0,), (0,))), preferred_elem...  2.4 us
    dot_general x1, matrix products, kernel_body(): lax.dot_general(select, summed, (((0,), (0,)), ((), ())), precision=lax.P...  1.85 us
    another operation x3, local copies, waits for them, and re-layouts, kernel_body(): left = jnp.stack([x_all, x_all, grad_all])  1.77 us
    dot_general x1, matrix products, kernel_body(): x_rows = jnp.dot(picker, tokens, preferred_element_type=jnp.float32)  1.4 us
    reduce_sum x1, other arithmetic, route_slots(): jnp.sum(jnp.where(hits, block_probs.astype(jnp.float32)[:, :, None], jnp....  0.8 us

profile of v3, /device:TPU:0, one launch (start us, length us, event | category | flops | bytes accessed | tf_op | source)
XLA Modules:
  0.0 36.3 jit_solution(7886144324227642651)
XLA Ops:
  0.6 0.0 copy-start
  0.6 0.8 %select_reduce_fusion = (f32[128]{0:T(128)S(1)}, pred[128,8]{0,1:T(8,128)(4,1)S(1)}) fusion(bf16[128,8]{0,1:T(8,128)(2,1)} %param.9, s32[128,8]{0,1:T(8,128)} %param.10), kind=kLoop, calls=%fused_computation.18 | loop fusion | flops 3968 | bytes 7680 | tf_op jit(solution)/shard_map/reduce_sum | solution.py:18
  1.5 0.1 copy.13
  1.6 0.2 reduce-window.7
  1.8 0.1 reduce.4
  1.9 0.1 convolution_bitcast_fusion
  2.0 0.0 copy-done
  2.0 0.2 fusion
  2.2 1.4 %convolution_convert_fusion.1 = bf16[8,3584]{1,0:T(8,128)(2,1)S(1)} fusion(bf16[128,3584]{1,0:T(8,128)(2,1)} %param.7, s32[128]{0:T(128)S(1)} %convert_subtract_fusion, pred[128]{0:T(512)(128)(4,1)S(1)} %get-tuple-element.14), kind=kOutput, calls=%fused_computation.3 | convolution fusion | flops 7372800 | bytes 975488 | tf_op jit(solution)/shard_map/dot_general | solution.py:329
  3.6 0.7 %pad_maximum_fusion.own = bf16[16,3584]{1,0:T(8,128)(2,1)} fusion(bf16[8,3584]{1,0:T(8,128)(2,1)S(1)} %fusion, bf16[8,3584]{1,0:T(8,128)(2,1)S(1)} %convolution_convert_fusion.1), kind=kLoop, calls=%fused_computation.14 | loop fusion | flops 229376 | bytes 229376 | tf_op jit(solution)/shard_map/concatenate | solution.py:331
  4.3 25.9 %shard_map.86 = (bf16[16,16,1792]{2,1,0:T(8,128)(2,1)}, bf16[2,3,64,256]{3,2,1,0:T(8,128)(2,1)}, f32[16,1792]{1,0:T(8,128)}) custom-call(bf16[16,3584]{1,0:T(8,128)(2,1)} %pad_maximum_fusion.own, bf16[1,3584,256]{2,1,0:T(8,128)(2,1)} %wg_hbm.1, bf16[1,3584,256]{2,1,0:T(8,128)(2,1)} %wu_hbm.1, bf16[1,256,3584]{2,1,0:T(8,128)(2,1)} %wd_hbm.1), custom_call_target="tpu_custom_call" | custom-call | tf_op jit(solution)/shard_map/pallas_call | solution.py:287
  30.2 0.0 copy-start.1
  30.3 1.3 %slice_bitcast_fusion.1 = (bf16[1,128,1792]{2,1,0:T(8,128)(2,1)S(1)}, bf16[1,128,1792]{2,1,0:T(8,128)(2,1)S(1)}) fusion(bf16[16,16,1792]{2,1,0:T(8,128)(2,1)} %get-tuple-element.6), kind=kLoop, calls=%fused_computation.13 | loop fusion | bytes 1835008 | tf_op jit(solution)/shard_map/stack;reshape | solution.py:343
  31.5 0.3 copy.14
  31.8 0.3 copy.16
  32.0 0.0 copy-done.1
  32.1 0.0 copy-start.2
  32.1 2.4 %fusion.1 = bf16[1,3,1792,256]{3,2,1,0:T(8,128)(2,1)} fusion(bf16[3,128,256]{2,1,0:T(8,128)(2,1)S(1)} %bitcast.19, bf16[1,128,1792]{1,2,0:T(8,128)(2,1)S(1)} %copy.16, bf16[1,128,1792]{1,2,0:T(8,128)(2,1)S(1)} %copy.14), kind=kOutput, calls=%fused_computation.5 | convolution fusion | flops 355074048 | bytes 3866624 | tf_op jit(solution)/shard_map/dot_general | solution.py:345
  34.5 0.0 copy-done.2
  34.5 1.8 %convolution_convert_fusion = bf16[128,3584]{1,0:T(8,128)(2,1)} fusion(f32[8,1792]{1,0:T(8,128)S(1)} %get-tuple-element.13, f32[8,1792]{1,0:T(8,128)S(1)} %get-tuple-element.12, s32[128]{0:T(128)S(1)} %convert_subtract_fusion, pred[128]{0:T(512)(128)(4,1)S(1)} %get-tuple-element.14), kind=kOutput, calls=%fused_computation | convolution fusion | flops 44529664 | bytes 1032832 | tf_op jit(solution)/shard_map/dot_general | solution.py:334
  (5 shorter events, 0.1 us)
Async XLA Ops:
  0.6 1.4 %copy-start = (bf16[128,3584]{1,0:T(8,128)(2,1)S(1)}, bf16[128,3584]{1,0:T(8,128)(2,1)}, u32[]{:S(2)}) copy-start(bf16[128,3584]{1,0:T(8,128)(2,1)} %param.8) | copy-start | bytes 2752516
  30.2 1.8 %copy-start.1 = (bf16[2,3,64,256]{3,2,1,0:T(8,128)(2,1)S(1)}, bf16[2,3,64,256]{3,2,1,0:T(8,128)(2,1)}, u32[]{:S(2)}) copy-start(bf16[2,3,64,256]{3,2,1,0:T(8,128)(2,1)} %get-tuple-element.7) | copy-start | bytes 589828
  32.1 2.4 %copy-start.2 = (f32[16,1792]{1,0:T(8,128)S(1)}, f32[16,1792]{1,0:T(8,128)}, u32[]{:S(2)}) copy-start(f32[16,1792]{1,0:T(8,128)} %get-tuple-element.5) | copy-start | bytes 344068
